TPU v7x, 256 devices: a whole 4x4x8 slice. The times are simulated.
256 devices in a mesh: seq: 16 (over x, y_hi, core), dp: 16 (over z, y_lo).
Axes of the slice: x: 4, y: 4 (y_hi: 2, y_lo: 2; y = y_hi * 2 + y_lo), z: 8, core: 2. Of those that a mesh axis runs over, the one named last changes fastest.
Arguments:
- frames: bfloat16 [16, 2048, 1024], P('dp', 'seq'), may hold values from -6 to 6
- lengths: int32 [16], P('dp'), may hold values from 1024 to 2048, as said below
- stretch_sizes: int32 [16], P('dp'), may hold values from 8 to 32, as said below
- look_ahead: int32 [16], P('dp'), may hold values from 1 to 8, as said below
- norm_one: float32 [1024], replicated, may hold values from 0.5 to 1.5
- norm_two: float32 [1024], replicated, may hold values from 0.5 to 1.5
- w_query: bfloat16 [1024, 1024], replicated, may hold values from -8 to 8
- w_key: bfloat16 [1024, 1024], replicated, may hold values from -1 to 1
- w_value: bfloat16 [1024, 1024], replicated, may hold values from -0.1875 to 0.1875
- w_out: bfloat16 [1024, 1024], replicated, may hold values from -0.1875 to 0.1875
- conv_kernel: bfloat16 [31, 1024], replicated, may hold values from -1 to 1
Outputs:
- full_output: bfloat16 [16, 2048, 1024], P('dp', 'seq')
- stretch_output: bfloat16 [16, 2048, 1024], P('dp', 'seq')
- kernel_grad: float32 [31, 1024], replicated
Inputs may be any that keep to these rules, and one draw needn't show every extreme that they name: `lengths`: utterance 0 has all 2048 frames. `stretch_sizes`: utterance 0 has stretch size 32. `look_ahead`: utterance 0 has preview 8.
All inputs are finite; a program needn't handle non-finite values.
Results may differ from a plain program's by a relative error of at most 0.0045.
The roundings to bfloat16 on the way count: a program that leaves them out, or rounds other values in their place, can miss the bound.
Values may be sent and summed in bfloat16 or wider, within the bound.
No kernel may reach another device: no remote copies, remote signals or barrier semaphores. Data moves between devices by JAX's collectives and lax.ppermute only.
A program may use at most 128 MiB of HBM per device.

v0:
```python
import math
import jax
import jax.numpy as jnp
from jax import lax
from jax.sharding import PartitionSpec as P

HEADS = 16
KERNEL = 31
LEFT = 64
HALO = 128
EPSILON = 1e-05
FLOOR_SCORE = -1e30


def with_halo(value, sides, width):
    for axis, dim in sides:
        size, length = (lax.axis_size(axis), value.shape[dim])
        up = [(i, (i + 1) % size) for i in range(size - 1)]
        down = [(j, i) for i, j in up]
        last = lax.slice_in_dim(value, length - width, length, axis=dim)
        leading = lax.slice_in_dim(value, 0, width, axis=dim)
        before = lax.ppermute(last, axis, up)
        after = lax.ppermute(leading, axis, down)
        value = jnp.concatenate([before, value, after], axis=dim)
    return value


def shifted(value, axis, by):
    length = lax.axis_size(axis)
    pairs = [(i, i + by) for i in range(length) if 0 <= i + by < length]
    return lax.ppermute(value, axis, pairs)


def layer_norm(values, gain_vector):
    values = values.astype(jnp.float32)
    center = values - jnp.mean(values, axis=-1, keepdims=True)
    spread = jnp.mean(center * center, axis=-1, keepdims=True)
    return center * lax.rsqrt(spread + EPSILON) * gain_vector


def fresh_state(row_count, head_count, depth_count):
    return (
        jnp.full((head_count, row_count), FLOOR_SCORE, jnp.float32),
        jnp.zeros((head_count, row_count), jnp.float32),
        jnp.zeros((row_count, head_count * depth_count), jnp.float32),
    )


def finish_state(state):
    highest, totals, summed = state
    row_count = summed.shape[0]
    head_count = totals.shape[0]
    mixed = summed.reshape(row_count, head_count, -1) / totals.T[:, :, None]
    return mixed.reshape(row_count, -1).astype(jnp.bfloat16)


def fold_keys(state, query3, query_pos, key3, value3, key_start, length, scale):
    highest, totals, summed = state
    key_count = key3.shape[0]
    scores = jnp.einsum("qhe,khe->hqk", query3, key3, preferred_element_type=jnp.float32) * scale
    key_pos = key_start + jnp.arange(key_count, dtype=jnp.int32)
    visible = (key_pos[None, :] < length) | (key_pos[None, :] == query_pos[:, None])
    scores = jnp.where(visible[None], scores, FLOOR_SCORE)
    new_high = jnp.maximum(highest, jnp.max(scores, axis=-1))
    factor = jnp.exp(highest - new_high)
    expo = jnp.where(visible[None], jnp.exp(scores - new_high[:, :, None]), 0.0)
    totals = totals * factor + jnp.sum(expo, axis=-1)
    adding = jnp.einsum(
        "hqk,khe->qhe", expo.astype(jnp.bfloat16), value3, preferred_element_type=jnp.float32
    )
    row_count, head_count, depth_count = adding.shape
    summed = summed.reshape(row_count, head_count, depth_count) * factor.T[:, :, None] + adding
    return (new_high, totals, summed.reshape(row_count, head_count * depth_count))


def fold_blocks(state, query3, query_pos, keys3, values3, length, scale):
    key_count = keys3.shape[0]
    block_width = math.gcd(key_count, 256)
    number = key_count // block_width
    key_blocks = keys3.reshape(number, block_width, keys3.shape[1], keys3.shape[2])
    value_blocks = values3.reshape(number, block_width, values3.shape[1], values3.shape[2])

    def advance(carry, inputs):
        index, key_block, value_block = inputs
        return (
            fold_keys(
                carry, query3, query_pos, key_block, value_block, index * block_width, length, scale
            ),
            None,
        )

    state, _ = lax.scan(
        advance, state, (jnp.arange(number, dtype=jnp.int32), key_blocks, value_blocks)
    )
    return state


def windowed(query3, key_ext3, value_ext3, first_pos, length, stretch, lookup, scale):
    query_count = query3.shape[0]
    block_rows = min(query_count, 512)
    number = query_count // block_rows
    span = block_rows + 2 * HALO

    def one_block(index):
        start = index * block_rows
        query_pos = first_pos + start + jnp.arange(block_rows, dtype=jnp.int32)
        key_pos = first_pos + start - HALO + jnp.arange(span, dtype=jnp.int32)
        begin = query_pos // stretch * stretch
        inside = (key_pos[None, :] >= begin[:, None] - LEFT) & (
            key_pos[None, :] < begin[:, None] + stretch + lookup
        )
        inside = inside & (key_pos[None, :] >= 0) & (key_pos[None, :] < length)
        visible = inside | (key_pos[None, :] == query_pos[:, None])
        scores = (
            jnp.einsum("qhe,khe->hqk", query3, key_ext3, preferred_element_type=jnp.float32) * scale
        )
        scores = jnp.where(visible[None], scores, FLOOR_SCORE)
        highest = jnp.max(scores, axis=-1, keepdims=True)
        expo = jnp.where(visible[None], jnp.exp(scores - highest), 0.0)
        totals = jnp.sum(expo, axis=-1)
        mixed = jnp.einsum(
            "hqk,khe->qhe",
            expo.astype(jnp.bfloat16),
            value_ext3,
            preferred_element_type=jnp.float32,
        )
        return (mixed / totals.T[:, :, None]).reshape(block_rows, -1).astype(jnp.bfloat16)

    return lax.map(one_block, jnp.arange(number, dtype=jnp.int32)).reshape(query_count, -1)


def per_device(
    frames,
    lengths,
    stretch_sizes,
    look_ahead,
    norm_one,
    norm_two,
    w_query,
    w_key,
    w_value,
    w_out,
    conv_kernel,
):
    source = frames[0]
    row_count, model_width = source.shape
    head_count = HEADS
    depth_count = model_width // head_count
    scale = float(depth_count) ** (-0.5)
    seq_place = lax.axis_index("seq")
    length = lengths[0]
    stretch = stretch_sizes[0]
    lookup = look_ahead[0]
    first_pos = seq_place * row_count
    query_pos = first_pos + jnp.arange(row_count, dtype=jnp.int32)
    normed = layer_norm(source, norm_one).astype(jnp.bfloat16)
    query = jnp.dot(normed, w_query, preferred_element_type=jnp.float32).astype(jnp.bfloat16)
    key_rows = jnp.dot(normed, w_key, preferred_element_type=jnp.float32).astype(jnp.bfloat16)
    value_rows = jnp.dot(normed, w_value, preferred_element_type=jnp.float32).astype(jnp.bfloat16)
    query3 = query.reshape(row_count, head_count, depth_count)
    key_piece = lax.all_gather(key_rows, "seq", axis=0, tiled=True)
    value_piece = lax.all_gather(value_rows, "seq", axis=0, tiled=True)
    piece_rows = key_piece.shape[0]
    state = fold_blocks(
        fresh_state(row_count, head_count, depth_count),
        query3,
        query_pos,
        key_piece.reshape(piece_rows, head_count, depth_count),
        value_piece.reshape(piece_rows, head_count, depth_count),
        length,
        scale,
    )
    context_full = finish_state(state)
    stacked = jnp.stack([key_rows, value_rows])
    extended = with_halo(stacked, (("seq", 1),), HALO)
    context_stretch = windowed(
        query3,
        extended[0].reshape(-1, head_count, depth_count),
        extended[1].reshape(-1, head_count, depth_count),
        first_pos,
        length,
        stretch,
        lookup,
        scale,
    )
    valid = (query_pos < length).astype(jnp.float32)
    kernel_taps = conv_kernel.astype(jnp.float32)
    projected = jnp.dot(
        jnp.concatenate([context_full, context_stretch], axis=0),
        w_out,
        preferred_element_type=jnp.float32,
    )
    residual_full = source.astype(jnp.float32) + projected[:row_count]
    residual_stretch = source.astype(jnp.float32) + projected[row_count:]
    input_full = (layer_norm(residual_full, norm_two) * valid[:, None]).astype(jnp.bfloat16)
    input_stretch = (layer_norm(residual_stretch, norm_two) * valid[:, None]).astype(jnp.bfloat16)
    padded_full = with_halo(input_full, (("seq", 0),), KERNEL // 2)
    carried = shifted(input_stretch[row_count - (KERNEL - 1) :], "seq", 1)
    padded_stretch = jnp.concatenate([carried, input_stretch], axis=0)
    conv_full = jnp.zeros((row_count, model_width), jnp.float32)
    conv_stretch = jnp.zeros((row_count, model_width), jnp.float32)
    for offset in range(KERNEL):
        conv_full = conv_full + kernel_taps[offset] * padded_full[
            offset : offset + row_count
        ].astype(jnp.float32)
        conv_stretch = conv_stretch + kernel_taps[offset] * padded_stretch[
            offset : offset + row_count
        ].astype(jnp.float32)
    output_full = residual_full + jax.nn.silu(conv_full)
    output_stretch = residual_stretch + jax.nn.silu(conv_stretch)
    push = (
        2.0 * (output_stretch - output_full) * valid[:, None] / jnp.sqrt(length.astype(jnp.float32))
    )
    sigma = jax.nn.sigmoid(conv_stretch)
    slope = push * sigma * (1.0 + conv_stretch * (1.0 - sigma))
    grad_local = jnp.stack(
        [
            jnp.sum(slope * padded_stretch[offset : offset + row_count].astype(jnp.float32), axis=0)
            for offset in range(KERNEL)
        ]
    )
    kernel_grad = lax.psum(grad_local, ("seq", "dp"))
    return (
        output_full.astype(jnp.bfloat16)[None],
        output_stretch.astype(jnp.bfloat16)[None],
        kernel_grad,
    )


def solution(mesh):
    in_specs = (P("dp", "seq", None), P("dp"), P("dp"), P("dp"), P(), P(), P(), P(), P(), P(), P())
    out_specs = (P("dp", "seq", None), P("dp", "seq", None), P())
    return jax.shard_map(
        per_device, mesh=mesh, in_specs=in_specs, out_specs=out_specs, check_vma=False
    )
```

profile of v0, /device:TPU:8, one launch (start us, length us, event | category | flops | bytes accessed | tf_op | source)
XLA Modules:
  0.0 529.4 jit_solution(953079403688141178)
XLA Ops:
  9.7 2.9 convolution_convert_fusion.2
  12.7 2.8 convolution_convert_fusion
  33.6 3.8 fusion.188
  37.4 2.9 fusion.36
  40.3 40.4 %all-gather.3.cloned.1.call-done = bf16[2048,1024]{1,0:T(8,128)(2,1)} async-done(((bf16[128,1024]{1,0:T(8,128)(2,1)}), bf16[2048,1024]{1,0:T(8,128)(2,1)}) %all-gather.3.cloned.1.call-update) | async-done | bytes 4194320 | tf_op jit(solution)/shard_map/all_gather | solution.py:161
  80.8 11.6 %reshape.276 = bf16[8,256,16,64]{3,2,1,0:T(8,128)(2,1)} reshape(bf16[2048,1024]{1,0:T(8,128)(2,1)} %all-gather.3.cloned.1.call-done) | data formatting | bytes 8388608 | tf_op jit(solution)/shard_map/reshape;reshape | solution.py:80
  92.3 10.4 %copy.25 = bf16[8,256,16,64]{1,3,2,0:T(8,128)(2,1)} copy(bf16[8,256,16,64]{3,2,1,0:T(8,128)(2,1)} %reshape.276) | data formatting | bytes 8388608
  102.7 41.3 %all-gather.5.cloned.1.call-done = bf16[2048,1024]{1,0:T(8,128)(2,1)} async-done(((bf16[128,1024]{1,0:T(8,128)(2,1)}), bf16[2048,1024]{1,0:T(8,128)(2,1)}) %all-gather.5.cloned.1.call-update) | async-done | bytes 4194320 | tf_op jit(solution)/shard_map/all_gather | solution.py:162
  144.0 11.6 %reshape.277 = bf16[8,256,16,64]{3,2,1,0:T(8,128)(2,1)} reshape(bf16[2048,1024]{1,0:T(8,128)(2,1)} %all-gather.5.cloned.1.call-done) | data formatting | bytes 8388608 | tf_op jit(solution)/shard_map/reshape;reshape | solution.py:81
  155.6 10.3 %copy.26 = bf16[8,256,16,64]{1,3,2,0:T(8,128)(2,1)} copy(bf16[8,256,16,64]{3,2,1,0:T(8,128)(2,1)} %reshape.277) | data formatting | bytes 8388608
  166.0 65.6 %while.5 = (s32[]{:T(128)}, f32[16,128]{1,0:T(8,128)S(1)}, f32[16,128]{1,0:T(8,128)S(1)}, f32[128,1024]{0,1:T(8,128)S(1)}, s32[8]{0:T(128)S(1)}, /*index=5*/s32[...) while((s32[]{:T(128)}, f32[16,128]{1,0:T(8,128)S(1)}, ...), condition=%wide.region_5.6_spmd.clone, body=%wide.region_2.5_spmd.clone.sunk | while | flops 141374336 | bytes 17306316 | solution.py:92
  168.0 2.9 fusion.211
  176.2 2.9 fusion.211
  184.4 2.9 fusion.211
  192.6 2.9 fusion.211
  195.6 2.6 fusion.215
  200.8 2.9 fusion.211
  209.0 2.9 fusion.211
  217.2 2.9 fusion.211
  225.4 2.9 fusion.211
  237.8 3.8 collective-permute-start.2
  245.1 21.2 %fusion.106 = (f32[1024]{0:T(1024)S(1)}, f32[1024]{0:T(1024)S(1)}, f32[1024]{0:T(1024)S(1)}, f32[1024]{0:T(1024)S(1)}, f32[1024]{0:T(1024)S(1)}, /*index=5*/f32[...) fusion(bf16[128,1024]{1,0:T(8,128)(2,1)} %copy-done.3, ...), kind=kLoop, calls=%fused_computation.235 | loop fusion | flops 57138176 | bytes 3432964 | tf_op jit(solution)/shard_map/reduce_sum | solution.py:218
  269.0 4.7 stack.139
  275.7 245.6 %all-reduce.2.cloned.1.call-done = f32[31,1024]{1,0:T(8,128)} async-done(((f32[31,1024]{1,0:T(8,128)}), f32[31,1024]{1,0:T(8,128)}) %all-reduce.2.cloned.1.call-update) | async-done | bytes 126992 | tf_op jit(solution)/shard_map/psum | solution.py:222
  (174 shorter events, 68.2 us)
Async XLA Ops:
  7.2 224.5 %copy-start = (bf16[1024,1024]{1,0:T(8,128)(2,1)S(1)}, bf16[1024,1024]{1,0:T(8,128)(2,1)}, u32[]{:S(2)}) copy-start(bf16[1024,1024]{1,0:T(8,128)(2,1)} %param.22) | copy-start | bytes 6291460
  7.2 5.5 %copy-start.2 = (bf16[1,128,1024]{2,1,0:T(8,128)(2,1)S(1)}, bf16[1,128,1024]{2,1,0:T(8,128)(2,1)}, u32[]{:S(2)}) copy-start(bf16[1,128,1024]{2,1,0:T(8,128)(2,1)} %param.13) | copy-start | bytes 786436
  7.2 5.5 %copy-start.10 = (f32[1024]{0:T(1024)S(1)}, f32[1024]{0:T(1024)}, u32[]{:S(2)}) copy-start(f32[1024]{0:T(1024)} %param.17) | copy-start | bytes 12292
  7.2 73.6 %all-gather.3.cloned.1.call-start = ((), (), s32[]{:S(2)}) async-start(), calls=%async_computation | async-start | bytes 4456448 | tf_op jit(solution)/shard_map/all_gather | solution.py:161
  12.6 3.0 copy-start.5
  12.6 131.4 %all-gather.5.cloned.1.call-start = ((), (), s32[]{:S(2)}) async-start(), calls=%async_computation.1 | async-start | bytes 4456448 | tf_op jit(solution)/shard_map/all_gather | solution.py:162
  15.5 505.8 %all-reduce.2.cloned.1.call-start = ((), (), s32[]{:S(2)}) async-start(), calls=%async_computation.2 | async-start | bytes 262144 | tf_op jit(solution)/shard_map/psum | solution.py:222
  15.5 10.9 %copy-start.9 = (bf16[31,1024]{1,0:T(8,128)(2,1)S(1)}, bf16[31,1024]{1,0:T(8,128)(2,1)}, u32[]{:S(2)}) copy-start(bf16[31,1024]{1,0:T(8,128)(2,1)} %param.23) | copy-start | bytes 190468
  15.5 12.3 %copy-start.6 = (bf16[128,1024]{1,0:T(8,128)(2,1)S(1)}, bf16[128,1024]{1,0:T(8,128)(2,1)}, u32[]{:S(2)}) copy-start(bf16[128,1024]{1,0:T(8,128)(2,1)} %convolution_convert_fusion) | copy-start | bytes 786436
  17.4 10.4 %collective-permute-start = (bf16[2,128,1024]{2,1,0:T(8,128)(2,1)}, bf16[2,128,1024]{2,1,0:T(8,128)(2,1)}, u32[]{:S(2)}, u32[]{:S(2)}) collective-permute-start(bf16[2,128,1024]{2,1,0:T(8,128)(2,1)} %pad_maximum_fusion.1), channel_id=1, source_target_pairs={{0,16},{16,32},{32,48},{48,64},{64,80},{80,96},{96,112},{112,128},... | collective-permute-start | bytes 1572872 | tf_op jit(solution)/shard_map/ppermute | solution.py:22
  20.0 7.8 %collective-permute-start.1 = (bf16[2,128,1024]{2,1,0:T(8,128)(2,1)}, bf16[2,128,1024]{2,1,0:T(8,128)(2,1)}, u32[]{:S(2)}, u32[]{:S(2)}) collective-permute-start(bf16[2,128,1024]{2,1,0:T(8,128)(2,1)} %pad_maximum_fusion.1), channel_id=1, source_target_pairs={{16,0},{32,16},{48,32},{64,48},{80,64},{96,80},{112,96},{128,112},... | collective-permute-start | bytes 1572872 | tf_op jit(solution)/shard_map/ppermute | solution.py:23
  33.6 3.8 copy-start.8
  171.0 2.6 copy-start.1
  179.2 2.6 copy-start.1
  187.4 2.6 copy-start.1
  195.6 2.6 copy-start.1
  203.8 2.6 copy-start.1
  220.2 2.6 copy-start.1
  228.4 2.6 copy-start.1
  234.3 2.9 copy-start.7
  235.0 10.0 %collective-permute-start.4 = (bf16[30,1024]{1,0:T(8,128)(2,1)S(1)}, bf16[30,1024]{1,0:T(8,128)(2,1)S(1)}, u32[]{:S(2)}, u32[]{:S(2)}) collective-permute-start(bf16[30,1024]{1,0:T(8,128)(2,1)S(1)} %slice.576), channel_id=1, source_target_pairs={{0,16},{16,32},{32,48},{48,64},{64,80},{80,96},{96,112},{112,128},... | collective-permute-start | bytes 184328 | tf_op jit(solution)/shard_map/ppermute | solution.py:31
  237.8 5.7 %collective-permute-start.2 = (bf16[15,1024]{1,0:T(8,128)(2,1)}, bf16[15,1024]{1,0:T(8,128)(2,1)}, u32[]{:S(2)}, u32[]{:S(2)}) collective-permute-start(bf16[15,1024]{1,0:T(8,128)(2,1)} %get-tuple-element.207), channel_id=1, source_target_pairs={{0,16},{16,32},{32,48},{48,64},{64,80},{80,96},{96,112},{112,128},... | collective-permute-start | bytes 92168 | tf_op jit(solution)/shard_map/ppermute | solution.py:22
  241.6 3.4 collective-permute-start.3
  243.5 22.7 %copy-start.4 = (bf16[128,1024]{1,0:T(8,128)(2,1)S(1)}, bf16[128,1024]{1,0:T(8,128)(2,1)}, u32[]{:S(2)}) copy-start(bf16[128,1024]{1,0:T(8,128)(2,1)} %copy-done.3) | copy-start | bytes 786436
  (4 other events, 4.7 us)
Sparse Core Ops, SparseCore 0:
  12.7 67.9 all-gather.2
  84.0 59.9 all-gather.4
  273.9 247.2 all-reduce.1
where the time goes:
time: 532 us; the launch traced here: 529 us
  waiting for transfers between devices  329 us (62%)
  local copies, waits for them, and re-layouts  62.4 us (12%)
  matrix products  60.6 us (11%)
  other arithmetic  44.4 us (8%)
  between operations  16.1 us (3%)
  starting transfers between devices  11.2 us (2%)
  loops' own time  5.82 us (1%)
    psum x1, waiting for transfers between devices, per_device(): kernel_grad = lax.psum(grad_local, ('seq', 'dp'))  246 us
    all_gather x1, waiting for transfers between devices, per_device(): value_piece = lax.all_gather(value_rows, 'seq', axis=0, tiled=True)  41.3 us
    all_gather x1, waiting for transfers between devices, per_device(): key_piece = lax.all_gather(key_rows, 'seq', axis=0, tiled=True)  40.4 us
    reduce_sum x4, other arithmetic, per_device(): jnp.sum(slope * padded_stretch[offset:offset + row_count].astype(jnp.floa...  24 us
    dot_general x8, matrix products, fold_keys(): jnp.einsum('qhe,khe->hqk', query3, key3, preferred_element_type=jnp.float32)  23.4 us
    unnamed x27, local copies, waits for them, and re-layouts  23.2 us
    dot_general x8, matrix products, fold_keys(): jnp.einsum('hqk,khe->qhe', expo.astype(jnp.bfloat16), value3, preferred_e...  21 us
    another operation x1, local copies, waits for them, and re-layouts, fold_blocks(): values3.reshape(number, block_width, values3.shape[1], values3.shape[2])  11.6 us
  transfers between devices with their start and end apart: 8, of which 4 were waited for; matrix products, arithmetic and copies ran while one was open for 9% of the time, Pallas kernels for 0%

commit v1 on v0

--- a/solution.py
+++ b/solution.py
@@ -219,7 +219,7 @@
             for offset in range(KERNEL)
         ]
     )
-    kernel_grad = lax.psum(grad_local, ("seq", "dp"))
+    kernel_grad = jnp.sum(jax.lax.all_gather(grad_local, axis_name=("seq", "dp")), 0)
     return (
         output_full.astype(jnp.bfloat16)[None],
         output_stretch.astype(jnp.bfloat16)[None],

time: 532 us -> 1040 us (1.95)
  the two profiles are of different devices: /device:TPU:8 before, /device:TPU:99 now
where the time goes in v1:
time: 1040 us
  waiting for transfers between devices  840 us (81%)
  local copies, waits for them, and re-layouts  60.2 us (6%)
  other arithmetic  57.5 us (6%)
  matrix products  43.2 us (4%)
  starting transfers between devices  16.9 us (2%)
  between operations  16.1 us (2%)
    all_gather x1, waiting for transfers between devices, per_device(): jax.lax.all_gather(grad_local, axis_name=('seq', 'dp'))  761 us
    all_gather x1, waiting for transfers between devices, per_device(): value_piece = lax.all_gather(value_rows, 'seq', axis=0, tiled=True)  41.3 us
    all_gather x1, waiting for transfers between devices, per_device(): key_piece = lax.all_gather(key_rows, 'seq', axis=0, tiled=True)  29.3 us
    reduce_sum x4, other arithmetic, per_device(): jnp.sum(slope * padded_stretch[offset:offset + row_count].astype(jnp.floa...  24.4 us
    unnamed x26, local copies, waits for them, and re-layouts  21.7 us
  transfers between devices with their start and end apart: 8, of which 6 were waited for; matrix products, arithmetic and copies ran while one was open for 4% of the time, Pallas kernels for 0%

profile of v1, /device:TPU:99, one launch (start us, length us, event | category | flops | bytes accessed | tf_op | source)
XLA Modules:
  0.0 1039.9 jit_solution(4578764949552929264)
XLA Ops:
  9.7 2.9 convolution_convert_fusion.2
  12.7 2.8 convolution_convert_fusion
  17.4 2.6 collective-permute-start.1
  20.0 4.7 collective-permute-start
  26.7 2.2 convolution_convert_fusion.1
  33.1 5.4 collective-permute-done
  40.9 2.3 copy.36
  44.4 3.8 fusion.188
  48.1 2.9 fusion.36
  51.0 29.3 %all-gather.6.cloned.1.call-done = bf16[2048,1024]{1,0:T(8,128)(2,1)} async-done(((bf16[128,1024]{1,0:T(8,128)(2,1)}), bf16[2048,1024]{1,0:T(8,128)(2,1)}) %all-gather.6.cloned.1.call-update) | async-done | bytes 4194320 | tf_op jit(solution)/shard_map/all_gather | solution.py:161
  80.3 11.6 %reshape.280 = bf16[8,256,16,64]{3,2,1,0:T(8,128)(2,1)} reshape(bf16[2048,1024]{1,0:T(8,128)(2,1)} %all-gather.6.cloned.1.call-done) | data formatting | bytes 8388608 | tf_op jit(solution)/shard_map/reshape;reshape | solution.py:80
  91.9 10.4 copy.33
  102.2 41.3 %all-gather.8.cloned.1.call-done = bf16[2048,1024]{1,0:T(8,128)(2,1)} async-done(((bf16[128,1024]{1,0:T(8,128)(2,1)}), bf16[2048,1024]{1,0:T(8,128)(2,1)}) %all-gather.8.cloned.1.call-update) | async-done | bytes 4194320 | tf_op jit(solution)/shard_map/all_gather | solution.py:162
  143.6 11.6 %reshape.281 = bf16[8,256,16,64]{3,2,1,0:T(8,128)(2,1)} reshape(bf16[2048,1024]{1,0:T(8,128)(2,1)} %all-gather.8.cloned.1.call-done) | data formatting | bytes 8388608 | tf_op jit(solution)/shard_map/reshape;reshape | solution.py:81
  155.2 10.3 copy.34
  165.5 48.2 %while.5 = (s32[]{:T(128)}, f32[16,128]{1,0:T(8,128)S(1)}, f32[16,128]{1,0:T(8,128)S(1)}, f32[128,1024]{0,1:T(8,128)S(1)}, s32[8]{0:T(128)S(1)}, /*index=5*/s32[...) while((s32[]{:T(128)}, f32[16,128]{1,0:T(8,128)S(1)}, ...), condition=%wide.region_5.6_spmd.clone, body=%wide.region_2.5_spmd.clone.sunk | while | flops 141374336 | bytes 8916672 | solution.py:92
  217.9 2.2 collective-permute-start.2
  220.1 2.3 collective-permute-start.3
  222.4 5.0 collective-permute-start.4
  228.9 21.6 %fusion.106 = (f32[1024]{0:T(1024)S(1)}, f32[1024]{0:T(1024)S(1)}, f32[1024]{0:T(1024)S(1)}, f32[1024]{0:T(1024)S(1)}, f32[1024]{0:T(1024)S(1)}, /*index=5*/f32[...) fusion(bf16[128,1024]{1,0:T(8,128)(2,1)} %copy-done.2, ...), kind=kLoop, calls=%fused_computation.235 | loop fusion | flops 57138176 | bytes 3432964 | tf_op jit(solution)/shard_map/reduce_sum | solution.py:218
  253.3 4.1 stack.139
  257.4 1.9 convert_bitcast_fusion.1
  259.3 761.3 %all-gather.10.cloned.1.call-done = f32[256,31,1024]{2,1,0:T(8,128)} async-done(((f32[1,31,1024]{2,1,0:T(8,128)}), f32[256,31,1024]{2,1,0:T(8,128)}) %all-gather.10.cloned.1.call-update) | async-done | bytes 32505872 | tf_op jit(solution)/shard_map/all_gather | solution.py:222
  1020.6 12.8 %reduce_sum.399 = f32[31,1024]{1,0:T(8,128)} reduce(f32[256,31,1024]{2,1,0:T(8,128)} %all-gather.10.cloned.1.call-done, f32[]{:T(128)} %constant.75.clone.1), dimensions={0}, to_apply=%region_43.44 | reduce | flops 8094720 | bytes 32632836 | tf_op jit(solution)/shard_map/reduce_sum | solution.py:222
  (158 shorter events, 62.8 us)
Async XLA Ops:
  7.2 206.6 %copy-start = (bf16[1024,1024]{1,0:T(8,128)(2,1)S(1)}, bf16[1024,1024]{1,0:T(8,128)(2,1)}, u32[]{:S(2)}) copy-start(bf16[1024,1024]{1,0:T(8,128)(2,1)} %param.22) | copy-start | bytes 6291460
  7.2 5.5 copy-start.1
  7.2 5.5 copy-start.9
  7.2 73.1 %all-gather.6.cloned.1.call-start = ((), (), s32[]{:S(2)}) async-start(), calls=%async_computation | async-start | bytes 4456448 | tf_op jit(solution)/shard_map/all_gather | solution.py:161
  12.6 3.0 copy-start.4
  12.6 131.0 %all-gather.8.cloned.1.call-start = ((), (), s32[]{:S(2)}) async-start(), calls=%async_computation.1 | async-start | bytes 4456448 | tf_op jit(solution)/shard_map/all_gather | solution.py:162
  15.5 1005.1 %all-gather.10.cloned.1.call-start = ((), (), s32[]{:S(2)}) async-start(), calls=%async_computation.2 | async-start | bytes 33685504 | tf_op jit(solution)/shard_map/all_gather | solution.py:222
  15.5 14.5 %copy-start.8 = (bf16[31,1024]{1,0:T(8,128)(2,1)S(1)}, bf16[31,1024]{1,0:T(8,128)(2,1)}, u32[]{:S(2)}) copy-start(bf16[31,1024]{1,0:T(8,128)(2,1)} %param.23) | copy-start | bytes 190468
  15.5 23.0 %copy-start.5 = (bf16[128,1024]{1,0:T(8,128)(2,1)S(1)}, bf16[128,1024]{1,0:T(8,128)(2,1)}, u32[]{:S(2)}) copy-start(bf16[128,1024]{1,0:T(8,128)(2,1)} %convolution_convert_fusion) | copy-start | bytes 786436
  17.4 15.7 %collective-permute-start.1 = (bf16[2,128,1024]{2,1,0:T(8,128)(2,1)}, bf16[2,128,1024]{2,1,0:T(8,128)(2,1)}, u32[]{:S(2)}, u32[]{:S(2)}) collective-permute-start(bf16[2,128,1024]{2,1,0:T(8,128)(2,1)} %pad_maximum_fusion.1), channel_id=1, source_target_pairs={{16,0},{32,16},{48,32},{64,48},{80,64},{96,80},{112,96},{128,112},... | collective-permute-start | bytes 1572872 | tf_op jit(solution)/shard_map/ppermute | solution.py:23
  20.0 18.6 %collective-permute-start = (bf16[2,128,1024]{2,1,0:T(8,128)(2,1)}, bf16[2,128,1024]{2,1,0:T(8,128)(2,1)}, u32[]{:S(2)}, u32[]{:S(2)}) collective-permute-start(bf16[2,128,1024]{2,1,0:T(8,128)(2,1)} %pad_maximum_fusion.1), channel_id=1, source_target_pairs={{0,16},{16,32},{32,48},{48,64},{64,80},{80,96},{96,112},{112,128},... | collective-permute-start | bytes 1572872 | tf_op jit(solution)/shard_map/ppermute | solution.py:22
  44.3 3.8 copy-start.7
  215.4 0.7 copy-start.10
  215.5 0.7 copy-start.11
  216.4 0.7 copy-start.2
  216.5 0.8 copy-start.6
  217.9 10.1 collective-permute-start.2
  220.1 7.9 collective-permute-start.3
  222.4 6.5 collective-permute-start.4
  228.0 22.5 %copy-start.3 = (bf16[128,1024]{1,0:T(8,128)(2,1)S(1)}, bf16[128,1024]{1,0:T(8,128)(2,1)}, u32[]{:S(2)}) copy-start(bf16[128,1024]{1,0:T(8,128)(2,1)} %copy-done.2) | copy-start | bytes 786436
Sparse Core Ops, SparseCore 0:
  12.7 67.5 all-gather.5
  83.6 59.9 all-gather.7
  257.5 763.0 all-gather.9
